TPU v7x, 512 devices: a whole 4x8x8 slice. The times are simulated.
512 devices in a mesh: sx: 32 (over y_lo, x, core), sy: 16 (over z, y_hi).
Axes of the slice: x: 4, y: 8 (y_hi: 2, y_lo: 4; y = y_hi * 4 + y_lo), z: 8, core: 2. Of those that a mesh axis runs over, the one named last changes fastest.
Arguments:
- schur_x: float32 [64, 16, 512, 512], P('sx', 'sy'), may hold values from -1 to 5, as said below
- schur_y: float32 [32, 32, 512, 512], P('sx', 'sy'), may hold values from -1 to 5, as said below
- residual_x: float32 [64, 16, 32, 512], P('sx', 'sy'), may hold values from -36 to 36
- residual_y: float32 [32, 32, 32, 512], P('sx', 'sy'), may hold values from -36 to 36
- basis_x: float32 [64, 16, 6, 512], P('sx', 'sy'), may hold values from -0.9 to 0.9
- basis_y: float32 [32, 32, 6, 512], P('sx', 'sy'), may hold values from -0.9 to 0.9
- couple_x: float32 [32, 16, 6, 6], P('sx', 'sy'), may hold values from -0.3 to 0.1
- couple_y: float32 [32, 16, 6, 6], P('sx', 'sy'), may hold values from -0.3 to 0.1
- coarse_shift: float32 [32, 16, 6], P('sx', 'sy'), may hold values from 0.05 to 0.5
Outputs:
- average_x: float32 [64, 16, 32, 512], P('sx', 'sy')
- average_y: float32 [32, 32, 32, 512], P('sx', 'sy')
- coarse_values: float32 [32, 16, 6, 32], P('sx', 'sy')
Inputs may be any that keep to these rules, and one draw needn't show every extreme that they name: `schur_x`: every block is symmetric positive definite. `schur_y`: every block is symmetric positive definite.
All inputs are finite; a program needn't handle non-finite values.
Results may differ from a plain program's by a relative error of at most 0.0003.
Values sent between devices are 32-bit elements; how exact they have to be, the bound alone decides.
A program may use at most 128 MiB of HBM per device.

v0:
```python
import jax
import jax.numpy as jnp
from jax import lax
from jax.sharding import PartitionSpec as P

CITERS = 8
HIGH = lax.Precision.HIGHEST


def shifted(array, axis, by):
    count = lax.axis_size(axis)
    pairs = [(i, i + by) for i in range(count) if 0 <= i + by < count]
    return lax.ppermute(array, axis, pairs)


def with_halo(cells, sides, width):
    for axis, dim in sides:
        count = lax.axis_size(axis)
        ends = count - 1
        head = lax.slice_in_dim(cells, 0, width, axis=dim)
        tail = lax.slice_in_dim(cells, cells.shape[dim] - width, cells.shape[dim], axis=dim)
        cells = jnp.concatenate(
            [
                lax.ppermute(tail, axis, [(i, (i + 1) % count) for i in range(ends)]),
                cells,
                lax.ppermute(head, axis, [((i + 1) % count, i) for i in range(ends)]),
            ],
            axis=dim,
        )
    return cells


def face_average(s_low, s_high, r_low, r_high):
    summed = s_low + s_high
    factor = jnp.linalg.cholesky(summed)
    right_side = jnp.dot(s_low, r_low.T, precision=HIGH) + jnp.dot(s_high, r_high.T, precision=HIGH)
    forward = jax.scipy.linalg.solve_triangular(factor, right_side, lower=True)
    solved = jax.scipy.linalg.solve_triangular(factor, forward, lower=True, trans=1)
    return solved.T


def shards(
    schur_x, schur_y, residual_x, residual_y, basis_x, basis_y, couple_x, couple_y, coarse_shift
):
    row_index = lax.axis_index("sx")
    row_count = lax.axis_size("sx")
    col_index = lax.axis_index("sy")
    col_count = lax.axis_size("sy")
    link_x = couple_x[0, 0] * (row_index > 0).astype(jnp.float32)
    link_y = couple_y[0, 0] * (col_index > 0).astype(jnp.float32)
    below_x = shifted((schur_x[1, 0], residual_x[1, 0]), "sx", 1)
    above_x = shifted((schur_x[0, 0], residual_x[0, 0], link_x), "sx", -1)
    below_y = shifted((schur_y[0, 1], residual_y[0, 1]), "sy", 1)
    above_y = shifted((schur_y[0, 0], residual_y[0, 0], link_y), "sy", -1)
    lower_x = face_average(below_x[0], schur_x[0, 0], below_x[1], residual_x[0, 0])
    upper_x = face_average(schur_x[1, 0], above_x[0], residual_x[1, 0], above_x[1])
    lower_y = face_average(below_y[0], schur_y[0, 0], below_y[1], residual_y[0, 0])
    upper_y = face_average(schur_y[0, 1], above_y[0], residual_y[0, 1], above_y[1])
    next_x = above_x[2]
    next_y = above_y[2]
    lower_x = jnp.where(row_index == 0, residual_x[0, 0], lower_x)
    upper_x = jnp.where(row_index == row_count - 1, residual_x[1, 0], upper_x)
    lower_y = jnp.where(col_index == 0, residual_y[0, 0], lower_y)
    upper_y = jnp.where(col_index == col_count - 1, residual_y[0, 1], upper_y)
    rhs_coarse = jnp.einsum("spf,srf->pr", basis_x[:, 0], residual_x[:, 0], precision=HIGH)
    rhs_coarse = rhs_coarse + jnp.einsum("spf,srf->pr", basis_y[0], residual_y[0], precision=HIGH)
    diagonal = (
        jnp.sum(jnp.abs(link_x), axis=0)
        + jnp.sum(jnp.abs(next_x), axis=1)
        + jnp.sum(jnp.abs(link_y), axis=0)
        + jnp.sum(jnp.abs(next_y), axis=1)
        + coarse_shift[0, 0]
    )
    coarse = jnp.zeros_like(rhs_coarse)
    remain = rhs_coarse

    def squares(values):
        return lax.psum(jnp.sum(values * values, axis=0), ("sx", "sy"))

    direction = rhs_coarse
    norm_now = squares(remain)
    for sweep_index in range(CITERS):
        padded = with_halo(direction[None, None], (("sx", 0), ("sy", 1)), 1)
        image = diagonal[:, None] * direction
        image = image + jnp.dot(link_x.T, padded[0, 1], precision=HIGH)
        image = image + jnp.dot(next_x, padded[2, 1], precision=HIGH)
        image = image + jnp.dot(link_y.T, padded[1, 0], precision=HIGH)
        image = image + jnp.dot(next_y, padded[1, 2], precision=HIGH)
        curve = lax.psum(jnp.sum(direction * image, axis=0), ("sx", "sy"))
        alpha = norm_now / curve
        coarse = coarse + alpha * direction
        remain = remain - alpha * image
        norm_next = squares(remain)
        direction = remain + norm_next / norm_now * direction
        norm_now = norm_next
    lift_x = jnp.einsum("pr,spf->srf", coarse, basis_x[:, 0], precision=HIGH)
    lift_y = jnp.einsum("pr,spf->srf", coarse, basis_y[0], precision=HIGH)
    out_x = (jnp.stack([lower_x, upper_x], axis=0) + lift_x)[:, None]
    out_y = (jnp.stack([lower_y, upper_y], axis=0) + lift_y)[None]
    return (out_x, out_y, coarse[None, None])


def solution(mesh):
    placed = (
        P("sx", "sy", None, None),
        P("sx", "sy", None, None),
        P("sx", "sy", None, None),
        P("sx", "sy", None, None),
        P("sx", "sy", None, None),
        P("sx", "sy", None, None),
        P("sx", "sy", None, None),
        P("sx", "sy", None, None),
        P("sx", "sy", None),
    )
    return jax.shard_map(
        shards,
        mesh=mesh,
        in_specs=placed,
        out_specs=(P("sx", "sy", None, None), P("sx", "sy", None, None), P("sx", "sy", None, None)),
        check_vma=False,
    )
```

profile of v0, /device:TPU:66, one launch (start us, length us, event | category | flops | bytes accessed | tf_op | source)
XLA Modules:
  0.0 2324.2 jit_solution(16223693384827084530)
XLA Ops:
  17.2 6.8 collective-permute-start.5
  33.9 7.5 collective-permute-start.9
  44.5 7.3 collective-permute-done.8
  52.2 110.4 %all-reduce.1 = (f32[32]{0:T(128)S(1)}, f32[32]{0:T(128)S(1)}) all-reduce(f32[32]{0:T(128)S(1)} %get-tuple-element.73, f32[32]{0:T(128)S(1)} %get-tuple-element.72), channel_id=1, replica_groups=mesh['sx'=32,'sy'=16] {'sx','sy'}, use_global_device_ids=true, to_apply=%region_9.13 | all-reduce | flops 64 | bytes 512 | tf_op jit(solution)/shard_map/psum | solution.py:78
  165.9 94.4 %psum.114 = f32[32]{0:T(128)S(1)} all-reduce(f32[32]{0:T(128)S(1)} %multiply_reduce_fusion.12), channel_id=1, replica_groups=mesh['sx'=32,'sy'=16] {'sx','sy'}, use_global_device_ids=true, to_apply=%region_17.21 | all-reduce | flops 32 | bytes 256 | tf_op jit(solution)/shard_map/psum | solution.py:78
  277.5 5.5 collective-permute-done.12
  283.4 96.4 %psum.115 = f32[32]{0:T(128)S(1)} all-reduce(f32[32]{0:T(128)S(1)} %get-tuple-element.183), channel_id=1, replica_groups=mesh['sx'=32,'sy'=16] {'sx','sy'}, use_global_device_ids=true, to_apply=%region_19.23 | all-reduce | flops 32 | bytes 256 | tf_op jit(solution)/shard_map/psum | solution.py:89
  379.9 95.0 %psum.116 = f32[32]{0:T(128)S(1)} all-reduce(f32[32]{0:T(128)S(1)} %get-tuple-element.116), channel_id=1, replica_groups=mesh['sx'=32,'sy'=16] {'sx','sy'}, use_global_device_ids=true, to_apply=%region_21.25 | all-reduce | flops 32 | bytes 256 | tf_op jit(solution)/shard_map/psum | solution.py:78
  492.1 5.8 collective-permute-done.16
  498.2 97.0 %psum.117 = f32[32]{0:T(128)S(1)} all-reduce(f32[32]{0:T(128)S(1)} %get-tuple-element.185), channel_id=1, replica_groups=mesh['sx'=32,'sy'=16] {'sx','sy'}, use_global_device_ids=true, to_apply=%region_23.27 | all-reduce | flops 32 | bytes 256 | tf_op jit(solution)/shard_map/psum | solution.py:89
  595.2 95.0 %psum.118 = f32[32]{0:T(128)S(1)} all-reduce(f32[32]{0:T(128)S(1)} %get-tuple-element.114), channel_id=1, replica_groups=mesh['sx'=32,'sy'=16] {'sx','sy'}, use_global_device_ids=true, to_apply=%region_25.29 | all-reduce | flops 32 | bytes 256 | tf_op jit(solution)/shard_map/psum | solution.py:78
  707.7 5.5 collective-permute-done.20
  713.7 97.1 %psum.119 = f32[32]{0:T(128)S(1)} all-reduce(f32[32]{0:T(128)S(1)} %get-tuple-element.187), channel_id=1, replica_groups=mesh['sx'=32,'sy'=16] {'sx','sy'}, use_global_device_ids=true, to_apply=%region_27.31 | all-reduce | flops 32 | bytes 256 | tf_op jit(solution)/shard_map/psum | solution.py:89
  810.8 95.5 %psum.120 = f32[32]{0:T(128)S(1)} all-reduce(f32[32]{0:T(128)S(1)} %get-tuple-element.112), channel_id=1, replica_groups=mesh['sx'=32,'sy'=16] {'sx','sy'}, use_global_device_ids=true, to_apply=%region_29.33 | all-reduce | flops 32 | bytes 256 | tf_op jit(solution)/shard_map/psum | solution.py:78
  929.6 97.1 %psum.121 = f32[32]{0:T(128)S(1)} all-reduce(f32[32]{0:T(128)S(1)} %get-tuple-element.189), channel_id=1, replica_groups=mesh['sx'=32,'sy'=16] {'sx','sy'}, use_global_device_ids=true, to_apply=%region_31.35 | all-reduce | flops 32 | bytes 256 | tf_op jit(solution)/shard_map/psum | solution.py:89
  1026.7 95.1 %psum.122 = f32[32]{0:T(128)S(1)} all-reduce(f32[32]{0:T(128)S(1)} %get-tuple-element.110), channel_id=1, replica_groups=mesh['sx'=32,'sy'=16] {'sx','sy'}, use_global_device_ids=true, to_apply=%region_33.37 | all-reduce | flops 32 | bytes 256 | tf_op jit(solution)/shard_map/psum | solution.py:78
  1128.9 5.4 collective-permute-start.29
  1138.9 5.8 collective-permute-done.28
  1145.8 97.0 %psum.123 = f32[32]{0:T(128)S(1)} all-reduce(f32[32]{0:T(128)S(1)} %get-tuple-element.191), channel_id=1, replica_groups=mesh['sx'=32,'sy'=16] {'sx','sy'}, use_global_device_ids=true, to_apply=%region_35.39 | all-reduce | flops 32 | bytes 256 | tf_op jit(solution)/shard_map/psum | solution.py:89
  1242.9 95.0 %psum.124 = f32[32]{0:T(128)S(1)} all-reduce(f32[32]{0:T(128)S(1)} %get-tuple-element.108), channel_id=1, replica_groups=mesh['sx'=32,'sy'=16] {'sx','sy'}, use_global_device_ids=true, to_apply=%region_37.41 | all-reduce | flops 32 | bytes 256 | tf_op jit(solution)/shard_map/psum | solution.py:78
  1355.1 5.8 collective-permute-done.32
  1361.9 97.1 %psum.125 = f32[32]{0:T(128)S(1)} all-reduce(f32[32]{0:T(128)S(1)} %get-tuple-element.193), channel_id=1, replica_groups=mesh['sx'=32,'sy'=16] {'sx','sy'}, use_global_device_ids=true, to_apply=%region_39.43 | all-reduce | flops 32 | bytes 256 | tf_op jit(solution)/shard_map/psum | solution.py:89
  1459.0 95.0 %psum.126 = f32[32]{0:T(128)S(1)} all-reduce(f32[32]{0:T(128)S(1)} %multiply_reduce_fusion), channel_id=1, replica_groups=mesh['sx'=32,'sy'=16] {'sx','sy'}, use_global_device_ids=true, to_apply=%region_41.45 | all-reduce | flops 32 | bytes 256 | tf_op jit(solution)/shard_map/psum | solution.py:78
  1565.8 5.4 collective-permute-start.37
  1575.3 5.7 collective-permute-start.36
  1590.9 131.7 %psum.127 = f32[32]{0:T(128)S(1)} all-reduce(f32[32]{0:T(128)S(1)} %fusion.30), channel_id=1, replica_groups=mesh['sx'=32,'sy'=16] {'sx','sy'}, use_global_device_ids=true, to_apply=%region_43.47 | all-reduce | flops 32 | bytes 256 | tf_op jit(solution)/shard_map/psum | solution.py:89
  1723.2 6.1 collective-permute-start.39
  1732.6 11.7 cholesky.462
  1744.5 9.8 custom-call.41
  1756.8 11.7 cholesky.481
  1768.6 10.2 custom-call.42
  1780.4 11.7 cholesky.502
  1792.1 9.8 custom-call.43
  1803.4 11.7 cholesky.519
  1820.1 7.7 while.16
  1827.8 39.3 %custom-call.45 = f32[4,128,128]{1,2,0:T(8,128)S(1)} custom-call(f32[4,128,128]{2,1,0:T(8,128)S(1)} %get-tuple-element.59), custom_call_target="InvertDiagBlocksLowerTriangular" | custom-call | tf_op jit(solution)/shard_map/jit(_solve_triangular)/triangular_solve | solution.py:38
  1876.9 7.1 collective-permute-start.41
  1889.2 11.7 cholesky.534
  1901.1 9.8 custom-call.46
  1913.4 11.7 cholesky.553
  1925.2 10.2 custom-call.47
  1936.9 11.7 cholesky.574
  1948.7 9.8 custom-call.48
  1960.0 11.7 cholesky.591
  1977.4 11.0 while.17
  1990.0 40.7 %custom-call.50 = f32[4,128,128]{1,2,0:T(8,128)} custom-call(f32[4,128,128]{2,1,0:T(8,128)} %get-tuple-element.61), custom_call_target="InvertDiagBlocksLowerTriangular" | custom-call | tf_op jit(solution)/shard_map/jit(_solve_triangular)/triangular_solve | solution.py:38
  2042.4 11.7 cholesky.606
  2054.2 9.8 custom-call.51
  2064.7 12.1 cholesky.625
  2076.9 9.8 custom-call.52
  2087.3 11.7 cholesky.646
  2099.1 9.8 custom-call.53
  2109.5 11.9 cholesky.663
  2126.2 7.8 while.18
  2135.7 39.3 %custom-call.55 = f32[4,128,128]{1,2,0:T(8,128)S(1)} custom-call(f32[4,128,128]{2,1,0:T(8,128)S(1)} %get-tuple-element.63), custom_call_target="InvertDiagBlocksLowerTriangular" | custom-call | tf_op jit(solution)/shard_map/jit(_solve_triangular)/triangular_solve | solution.py:38
  2184.5 11.7 cholesky.678
  2196.4 9.8 custom-call.56
  2206.9 11.9 cholesky.697
  2218.8 9.8 custom-call.57
  2229.3 11.7 cholesky.718
  2241.1 9.8 custom-call.58
  2251.5 12.1 cholesky.735
  2268.4 8.1 while.19
  2277.6 39.3 %custom-call.60 = f32[4,128,128]{1,2,0:T(8,128)S(1)} custom-call(f32[4,128,128]{2,1,0:T(8,128)S(1)} %get-tuple-element.65), custom_call_target="InvertDiagBlocksLowerTriangular" | custom-call | tf_op jit(solution)/shard_map/jit(_solve_triangular)/triangular_solve | solution.py:38
  (439 shorter events, 276.5 us)
Async XLA Ops:
  3.7 30.2 %collective-permute-start.7 = (f32[1,1,6,32]{3,2,1,0:T(8,128)S(1)}, f32[1,1,6,32]{3,2,1,0:T(8,128)S(1)}, u32[]{:S(2)}, u32[]{:S(2)}) collective-permute-start(f32[1,1,6,32]{3,2,1,0:T(8,128)S(1)} %bitcast.543), channel_id=1, source_target_pairs={{16,0},{32,16},{48,32},{64,48},{80,64},{96,80},{112,96},{128,112},... | collective-permute-start | bytes 2312 | tf_op jit(solution)/shard_map/ppermute | solution.py:26
  5.6 28.3 %collective-permute-start.6 = (f32[1,1,6,32]{3,2,1,0:T(8,128)S(1)}, f32[1,1,6,32]{3,2,1,0:T(8,128)S(1)}, u32[]{:S(2)}, u32[]{:S(2)}) collective-permute-start(f32[1,1,6,32]{3,2,1,0:T(8,128)S(1)} %bitcast.544), channel_id=1, source_target_pairs={{0,16},{16,32},{32,48},{48,64},{64,80},{80,96},{96,112},{112,128},... | collective-permute-start | bytes 2312 | tf_op jit(solution)/shard_map/ppermute | solution.py:24
  9.7 14.3 copy-start.28
  9.8 24.1 %copy-start.33 = (f32[1,1,6]{2,1,0:T(1,128)S(1)}, f32[1,1,6]{2,1,0:T(1,128)}, u32[]{:S(2)}) copy-start(f32[1,1,6]{2,1,0:T(1,128)} %param.22) | copy-start | bytes 76
  11.1 1712.1 %collective-permute-start = (f32[512,512]{0,1:T(8,128)}, f32[512,512]{0,1:T(8,128)}, u32[]{:S(2)}, u32[]{:S(2)}) collective-permute-start(f32[512,512]{0,1:T(8,128)} %bitcast.1), channel_id=1, source_target_pairs={{0,16},{16,32},{32,48},{48,64},{64,80},{80,96},{96,112},{112,128},... | collective-permute-start | bytes 3145736 | tf_op jit(solution)/shard_map/ppermute | solution.py:13
  14.8 1852.4 %collective-permute-start.1 = (f32[32,512]{1,0:T(8,128)}, f32[32,512]{1,0:T(8,128)}, u32[]{:S(2)}, u32[]{:S(2)}) collective-permute-start(f32[32,512]{1,0:T(8,128)} %get-tuple-element.136), channel_id=1, source_target_pairs={{0,16},{16,32},{32,48},{48,64},{64,80},{80,96},{96,112},{112,128},... | collective-permute-start | bytes 196616 | tf_op jit(solution)/shard_map/ppermute | solution.py:13
  17.2 9.4 collective-permute-start.5
  26.6 3.5 collective-permute-start.4
  30.1 1846.8 %collective-permute-start.2 = (f32[512,512]{0,1:T(8,128)}, f32[512,512]{0,1:T(8,128)S(1)}, u32[]{:S(2)}, u32[]{:S(2)}) collective-permute-start(f32[512,512]{0,1:T(8,128)} %bitcast.2), channel_id=1, source_target_pairs={{16,0},{32,16},{48,32},{64,48},{80,64},{96,80},{112,96},{128,112},... | collective-permute-start | bytes 3145736 | tf_op jit(solution)/shard_map/ppermute | solution.py:13
  33.8 679.6 %copy-start.34 = (f32[6]{0:T(128)}, f32[6]{0:T(128)S(1)}, u32[]{:S(2)}) copy-start(f32[6]{0:T(128)S(1)} %bitcast_add_fusion.4) | copy-start | bytes 76
  33.9 10.5 collective-permute-start.9
  41.4 10.4 collective-permute-start.8
  162.6 217.2 %copy-start.29 = (f32[32]{0:T(128)}, f32[32]{0:T(128)S(1)}, u32[]{:S(2)}) copy-start(f32[32]{0:T(128)S(1)} %div.51) | copy-start | bytes 388
  162.6 102.0 %copy-start = (f32[2,1,512,512]{3,2,1,0:T(8,128)S(1)}, f32[2,1,512,512]{3,2,1,0:T(8,128)}, u32[]{:S(2)}) copy-start(f32[2,1,512,512]{3,2,1,0:T(8,128)} %param.14) | copy-start | bytes 6291460
  165.9 528.8 %copy-start.7 = (f32[1,2,32,512]{3,2,1,0:T(8,128)S(1)}, f32[1,2,32,512]{3,2,1,0:T(8,128)}, u32[]{:S(2)}) copy-start(f32[1,2,32,512]{3,2,1,0:T(8,128)} %param.17) | copy-start | bytes 393220
  260.3 6.1 collective-permute-start.11
  262.5 4.9 collective-permute-start.10
  267.5 9.9 collective-permute-start.13
  272.5 10.5 collective-permute-start.12
  379.9 101.1 %copy-start.31 = (f32[32]{0:T(128)}, f32[32]{0:T(128)S(1)}, u32[]{:S(2)}) copy-start(f32[32]{0:T(128)S(1)} %div.53) | copy-start | bytes 388
  474.9 6.0 collective-permute-start.15
  477.1 4.9 collective-permute-start.14
  482.1 9.9 collective-permute-start.17
  487.4 10.5 collective-permute-start.16
  690.3 7.3 collective-permute-start.19
  692.5 5.1 collective-permute-start.18
  697.6 863.4 %copy-start.3 = (f32[1,1,512,512]{3,2,1,0:T(8,128)S(1)}, f32[1,1,512,512]{3,2,1,0:T(8,128)}, u32[]{:S(2)}) copy-start(f32[1,1,512,512]{3,2,1,0:T(8,128)} %get-tuple-element.127) | copy-start | bytes 3145732
  697.6 10.0 collective-permute-start.21
  702.6 10.6 collective-permute-start.20
  906.4 6.6 collective-permute-start.23
  908.3 4.9 collective-permute-start.22
  913.2 9.9 collective-permute-start.25
  918.1 10.4 collective-permute-start.24
  1121.9 5.0 collective-permute-start.27
  1124.0 4.9 collective-permute-start.26
  1128.9 9.9 collective-permute-start.29
  1134.3 10.5 collective-permute-start.28
  1337.9 4.9 collective-permute-start.31
  1340.1 4.9 collective-permute-start.30
  1345.0 9.9 collective-permute-start.33
  1350.4 10.5 collective-permute-start.32
  1554.0 8.3 collective-permute-start.35
  1556.2 9.5 collective-permute-start.34
  1558.4 32.3 %copy-start.35 = (f32[6]{0:T(128)S(1)}, f32[6]{0:T(128)}, u32[]{:S(2)}) copy-start(f32[6]{0:T(128)} %copy-done.34) | copy-start | bytes 76
  1558.4 164.2 %copy-start.30 = (f32[32]{0:T(128)S(1)}, f32[32]{0:T(128)}, u32[]{:S(2)}) copy-start(f32[32]{0:T(128)} %copy-done.29) | copy-start | bytes 388
  1558.4 164.2 %copy-start.32 = (f32[32]{0:T(128)S(1)}, f32[32]{0:T(128)}, u32[]{:S(2)}) copy-start(f32[32]{0:T(128)} %copy-done.31) | copy-start | bytes 388
  1562.4 468.4 %collective-permute-start.3 = (f32[32,512]{1,0:T(8,128)}, f32[32,512]{1,0:T(8,128)}, u32[]{:S(2)}, u32[]{:S(2)}) collective-permute-start(f32[32,512]{1,0:T(8,128)} %get-tuple-element.137), channel_id=1, source_target_pairs={{16,0},{32,16},{48,32},{64,48},{80,64},{96,80},{112,96},{128,112},... | collective-permute-start | bytes 196616 | tf_op jit(solution)/shard_map/ppermute | solution.py:13
  1565.8 9.5 collective-permute-start.37
  1575.3 10.4 collective-permute-start.36
  1585.7 454.7 %collective-permute-start.38 = (f32[512,512]{0,1:T(8,128)}, f32[512,512]{0,1:T(8,128)}, u32[]{:S(2)}, u32[]{:S(2)}) collective-permute-start(f32[512,512]{0,1:T(8,128)} %bitcast.92), channel_id=1, source_target_pairs={{0,1},{1,2},{2,3},{3,4},{4,5},{5,6},{6,7},{7,8},{8,9},{9,10},{10,1... | collective-permute-start | bytes 3145736 | tf_op jit(solution)/shard_map/ppermute | solution.py:13
  1723.2 451.8 %collective-permute-start.39 = (f32[32,512]{1,0:T(8,128)}, f32[32,512]{1,0:T(8,128)}, u32[]{:S(2)}, u32[]{:S(2)}) collective-permute-start(f32[32,512]{1,0:T(8,128)} %get-tuple-element.132), channel_id=1, source_target_pairs={{0,1},{1,2},{2,3},{3,4},{4,5},{5,6},{6,7},{7,8},{8,9},{9,10},{10,1... | collective-permute-start | bytes 196616 | tf_op jit(solution)/shard_map/ppermute | solution.py:13
  1768.6 51.5 %copy-start.36 = (s32[4]{0:T(128)S(1)}, s32[4]{0:T(128)}, u32[]{:S(2)}) copy-start(s32[4]{0:T(128)} %iota_multiply_fusion) | copy-start | bytes 52
  1867.2 315.0 %collective-permute-start.40 = (f32[512,512]{0,1:T(8,128)}, f32[512,512]{0,1:T(8,128)}, u32[]{:S(2)}, u32[]{:S(2)}) collective-permute-start(f32[512,512]{0,1:T(8,128)} %bitcast.538), channel_id=1, source_target_pairs={{1,0},{2,1},{3,2},{4,3},{5,4},{6,5},{7,6},{8,7},{9,8},{10,9},{11,1... | collective-permute-start | bytes 3145736 | tf_op jit(solution)/shard_map/ppermute | solution.py:13
  1876.9 440.0 %collective-permute-start.41 = (f32[32,512]{1,0:T(8,128)}, f32[32,512]{1,0:T(8,128)}, u32[]{:S(2)}, u32[]{:S(2)}) collective-permute-start(f32[32,512]{1,0:T(8,128)} %get-tuple-element.133), channel_id=1, source_target_pairs={{1,0},{2,1},{3,2},{4,3},{5,4},{6,5},{7,6},{8,7},{9,8},{10,9},{11,1... | collective-permute-start | bytes 196616 | tf_op jit(solution)/shard_map/ppermute | solution.py:13
  1977.4 63.0 %copy-start.2 = (f32[1,1,512,512]{2,3,1,0:T(8,128)S(1)}, f32[1,1,512,512]{2,3,1,0:T(8,128)}, u32[]{:S(2)}) copy-start(f32[1,1,512,512]{2,3,1,0:T(8,128)} %copy.46) | copy-start | bytes 3145732
  2126.1 52.9 %copy-start.27 = (f32[128,32]{0,1:T(8,128)S(1)}, f32[128,32]{0,1:T(8,128)}, u32[]{:S(2)}) copy-start(f32[128,32]{0,1:T(8,128)} %convolution_subtract_fusion.6) | copy-start | bytes 49156
  2268.4 53.6 %copy-start.13 = (f32[128,32]{0,1:T(8,128)S(1)}, f32[128,32]{0,1:T(8,128)}, u32[]{:S(2)}) copy-start(f32[128,32]{0,1:T(8,128)} %copy-done.12) | copy-start | bytes 49156
  2268.4 53.6 %copy-start.15 = (f32[128,32]{0,1:T(8,128)S(1)}, f32[128,32]{0,1:T(8,128)}, u32[]{:S(2)}) copy-start(f32[128,32]{0,1:T(8,128)} %copy-done.14) | copy-start | bytes 49156
  2268.4 53.6 %copy-start.20 = (f32[128,32]{0,1:T(8,128)S(1)}, f32[128,32]{0,1:T(8,128)}, u32[]{:S(2)}) copy-start(f32[128,32]{0,1:T(8,128)} %fusion.156) | copy-start | bytes 49156
  2268.4 53.6 %copy-start.22 = (f32[128,32]{0,1:T(8,128)S(1)}, f32[128,32]{0,1:T(8,128)}, u32[]{:S(2)}) copy-start(f32[128,32]{0,1:T(8,128)} %copy-done.21) | copy-start | bytes 49156
  2268.4 53.6 %copy-start.25 = (f32[128,32]{0,1:T(8,128)S(1)}, f32[128,32]{0,1:T(8,128)}, u32[]{:S(2)}) copy-start(f32[128,32]{0,1:T(8,128)} %fusion.154) | copy-start | bytes 49156
  2268.4 53.6 %copy-start.26 = (f32[128,32]{0,1:T(8,128)S(1)}, f32[128,32]{0,1:T(8,128)}, u32[]{:S(2)}) copy-start(f32[128,32]{0,1:T(8,128)} %fusion.162) | copy-start | bytes 49156
  2276.5 46.5 %copy-start.17 = (f32[128,32]{0,1:T(8,128)S(1)}, f32[128,32]{0,1:T(8,128)}, u32[]{:S(2)}) copy-start(f32[128,32]{0,1:T(8,128)} %copy-done.16) | copy-start | bytes 49156
  2276.5 46.5 %copy-start.24 = (f32[128,32]{0,1:T(8,128)S(1)}, f32[128,32]{0,1:T(8,128)}, u32[]{:S(2)}) copy-start(f32[128,32]{0,1:T(8,128)} %copy-done.23) | copy-start | bytes 49156
  (15 other events, 78.2 us)
where the time goes:
time: 2340 us; the launch traced here: 2320 us
  blocking collectives  1490 us (64%)
  other arithmetic  485 us (21%)
  starting transfers between devices  159 us (7%)
  matrix products  65.3 us (3%)
  waiting for transfers between devices  58.6 us (3%)
  local copies, waits for them, and re-layouts  54.3 us (2%)
    psum x8, blocking collectives, squares(): return lax.psum(jnp.sum(values * values, axis=0), ('sx', 'sy'))  776 us
    psum x7, blocking collectives, shards(): curve = lax.psum(jnp.sum(direction * image, axis=0), ('sx', 'sy'))  713 us
    another operation x56, other arithmetic, face_average(): factor = jnp.linalg.cholesky(summed)  316 us
    another operation x9, other arithmetic, face_average(): jax.scipy.linalg.solve_triangular(factor, forward, lower=True, trans=1)  160 us
    ppermute x16, starting transfers between devices, with_halo(): lax.ppermute(head, axis, [((i + 1) % count, i) for i in range(ends)])  60.7 us
    ppermute x16, starting transfers between devices, with_halo(): lax.ppermute(tail, axis, [(i, (i + 1) % count) for i in range(ends)])  53.9 us
    ppermute x16, waiting for transfers between devices, with_halo(): lax.ppermute(tail, axis, [(i, (i + 1) % count) for i in range(ends)])  52.2 us
  transfers between devices with their start and end apart: 42, of which 16 were waited for; matrix products, arithmetic and copies ran while one was open for 25% of the time, Pallas kernels for 0%

commit v1 on v0

--- a/solution.py
+++ b/solution.py
@@ -86,7 +86,7 @@
         image = image + jnp.dot(next_x, padded[2, 1], precision=HIGH)
         image = image + jnp.dot(link_y.T, padded[1, 0], precision=HIGH)
         image = image + jnp.dot(next_y, padded[1, 2], precision=HIGH)
-        curve = lax.psum(jnp.sum(direction * image, axis=0), ("sx", "sy"))
+        curve = jnp.sum(lax.all_gather(jnp.sum(direction * image, axis=0), ("sx", "sy")), axis=0)
         alpha = norm_now / curve
         coarse = coarse + alpha * direction
         remain = remain - alpha * image

time: 2340 us -> 3590 us (1.53)
  the two profiles are of different devices: /device:TPU:66 before, /device:TPU:64 now
where the time goes in v1:
time: 3590 us; the launch traced here: 3580 us
  waiting for transfers between devices  2000 us (56%)
  blocking collectives  763 us (21%)
  other arithmetic  495 us (14%)
  starting transfers between devices  152 us (4%)
  local copies, waits for them, and re-layouts  72.6 us (2%)
  matrix products  67.3 us (2%)
    unnamed x16, waiting for transfers between devices  1940 us
    psum x8, blocking collectives, squares(): return lax.psum(jnp.sum(values * values, axis=0), ('sx', 'sy'))  763 us
    another operation x56, other arithmetic, face_average(): factor = jnp.linalg.cholesky(summed)  316 us
    another operation x9, other arithmetic, face_average(): jax.scipy.linalg.solve_triangular(factor, forward, lower=True, trans=1)  159 us
  transfers between devices with their start and end apart: 50, of which 21 were waited for; matrix products, arithmetic and copies ran while one was open for 17% of the time, Pallas kernels for 0%

profile of v1, /device:TPU:64, one launch (start us, length us, event | category | flops | bytes accessed | tf_op | source)
XLA Modules:
  0.0 3580.5 jit_solution(10021695588280885919)
XLA Ops:
  15.5 6.8 collective-permute-start.5
  27.2 7.1 collective-permute-start.9
  37.2 7.4 collective-permute-done.8
  47.4 104.0 %psum.56 = f32[32]{0:T(128)S(1)} all-reduce(f32[32]{0:T(128)S(1)} %get-tuple-element.73), channel_id=1, replica_groups=mesh['sx'=32,'sy'=16] {'sx','sy'}, use_global_device_ids=true, to_apply=%region_9.13 | all-reduce | flops 32 | bytes 256 | tf_op jit(solution)/shard_map/psum | solution.py:78
  151.4 158.1 %all-reduce.18.cloned.1.call-done = f32[16384]{0:T(1024)} async-done(((f32[16384]{0:T(1024)}), f32[16384]{0:T(1024)}) %all-reduce.18.cloned.1.call-update) | async-done | bytes 65552
  310.7 94.1 %psum.57 = f32[32]{0:T(128)S(1)} all-reduce(f32[32]{0:T(128)S(1)} %multiply_reduce_fusion.12), channel_id=1, replica_groups=mesh['sx'=32,'sy'=16] {'sx','sy'}, use_global_device_ids=true, to_apply=%region_17.21 | all-reduce | flops 32 | bytes 256 | tf_op jit(solution)/shard_map/psum | solution.py:78
  420.0 6.9 collective-permute-done.12
  429.6 255.6 %all-reduce.20.cloned.1.call-done = f32[16384]{0:T(1024)} async-done(((f32[16384]{0:T(1024)}), f32[16384]{0:T(1024)}) %all-reduce.20.cloned.1.call-update) | async-done | bytes 65552
  686.3 94.1 %psum.58 = f32[32]{0:T(128)S(1)} all-reduce(f32[32]{0:T(128)S(1)} %get-tuple-element.114), channel_id=1, replica_groups=mesh['sx'=32,'sy'=16] {'sx','sy'}, use_global_device_ids=true, to_apply=%region_21.25 | all-reduce | flops 32 | bytes 256 | tf_op jit(solution)/shard_map/psum | solution.py:78
  795.6 6.9 collective-permute-done.16
  803.9 255.6 %all-reduce.22.cloned.1.call-done = f32[16384]{0:T(1024)} async-done(((f32[16384]{0:T(1024)}), f32[16384]{0:T(1024)}) %all-reduce.22.cloned.1.call-update) | async-done | bytes 65552
  1060.7 94.1 %psum.59 = f32[32]{0:T(128)S(1)} all-reduce(f32[32]{0:T(128)S(1)} %get-tuple-element.112), channel_id=1, replica_groups=mesh['sx'=32,'sy'=16] {'sx','sy'}, use_global_device_ids=true, to_apply=%region_25.29 | all-reduce | flops 32 | bytes 256 | tf_op jit(solution)/shard_map/psum | solution.py:78
  1170.0 6.9 collective-permute-done.20
  1178.3 255.6 %all-reduce.24.cloned.1.call-done = f32[16384]{0:T(1024)} async-done(((f32[16384]{0:T(1024)}), f32[16384]{0:T(1024)}) %all-reduce.24.cloned.1.call-update) | async-done | bytes 65552
  1435.0 94.1 %psum.60 = f32[32]{0:T(128)S(1)} all-reduce(f32[32]{0:T(128)S(1)} %get-tuple-element.110), channel_id=1, replica_groups=mesh['sx'=32,'sy'=16] {'sx','sy'}, use_global_device_ids=true, to_apply=%region_29.33 | all-reduce | flops 32 | bytes 256 | tf_op jit(solution)/shard_map/psum | solution.py:78
  1541.3 6.5 collective-permute-start.25
  1551.3 6.9 collective-permute-done.24
  1565.4 247.6 %all-reduce.26.cloned.1.call-done = f32[16384]{0:T(1024)} async-done(((f32[16384]{0:T(1024)}), f32[16384]{0:T(1024)}) %all-reduce.26.cloned.1.call-update) | async-done | bytes 65552
  1815.9 94.1 %psum.61 = f32[32]{0:T(128)S(1)} all-reduce(f32[32]{0:T(128)S(1)} %get-tuple-element.108), channel_id=1, replica_groups=mesh['sx'=32,'sy'=16] {'sx','sy'}, use_global_device_ids=true, to_apply=%region_33.37 | all-reduce | flops 32 | bytes 256 | tf_op jit(solution)/shard_map/psum | solution.py:78
  1919.0 6.6 collective-permute-start.29
  1929.1 6.9 collective-permute-done.28
  1939.3 251.3 %all-reduce.28.cloned.1.call-done = f32[16384]{0:T(1024)} async-done(((f32[16384]{0:T(1024)}), f32[16384]{0:T(1024)}) %all-reduce.28.cloned.1.call-update) | async-done | bytes 65552
  2193.9 94.1 %psum.62 = f32[32]{0:T(128)S(1)} all-reduce(f32[32]{0:T(128)S(1)} %get-tuple-element.106), channel_id=1, replica_groups=mesh['sx'=32,'sy'=16] {'sx','sy'}, use_global_device_ids=true, to_apply=%region_37.41 | all-reduce | flops 32 | bytes 256 | tf_op jit(solution)/shard_map/psum | solution.py:78
  2304.8 6.9 collective-permute-done.32
  2316.6 251.8 %all-reduce.30.cloned.1.call-done = f32[16384]{0:T(1024)} async-done(((f32[16384]{0:T(1024)}), f32[16384]{0:T(1024)}) %all-reduce.30.cloned.1.call-update) | async-done | bytes 65552
  2571.8 94.1 %psum.63 = f32[32]{0:T(128)S(1)} all-reduce(f32[32]{0:T(128)S(1)} %multiply_reduce_fusion), channel_id=1, replica_groups=mesh['sx'=32,'sy'=16] {'sx','sy'}, use_global_device_ids=true, to_apply=%region_41.45 | all-reduce | flops 32 | bytes 256 | tf_op jit(solution)/shard_map/psum | solution.py:78
  2705.9 268.6 %all-reduce.32.cloned.1.call-done = f32[16384]{0:T(1024)} async-done(((f32[16384]{0:T(1024)}), f32[16384]{0:T(1024)}) %all-reduce.32.cloned.1.call-update) | async-done | bytes 65552
  2982.7 11.7 cholesky.462
  2994.6 9.8 custom-call.41
  3006.9 11.7 cholesky.481
  3018.7 10.2 custom-call.42
  3030.5 11.7 cholesky.502
  3042.3 9.8 custom-call.43
  3053.5 11.7 cholesky.519
  3070.1 7.6 while.16
  3077.7 39.3 %custom-call.45 = f32[4,128,128]{1,2,0:T(8,128)S(1)} custom-call(f32[4,128,128]{2,1,0:T(8,128)S(1)} %get-tuple-element.59), custom_call_target="InvertDiagBlocksLowerTriangular" | custom-call | tf_op jit(solution)/shard_map/jit(_solve_triangular)/triangular_solve | solution.py:38
  3117.0 8.7 collective-permute-start.40
  3139.0 11.7 cholesky.534
  3150.9 9.8 custom-call.46
  3163.3 11.7 cholesky.553
  3175.0 10.2 custom-call.47
  3186.8 11.7 cholesky.574
  3198.5 9.8 custom-call.48
  3209.8 11.7 cholesky.591
  3227.2 10.7 while.17
  3239.6 40.7 %custom-call.50 = f32[4,128,128]{1,2,0:T(8,128)} custom-call(f32[4,128,128]{2,1,0:T(8,128)} %get-tuple-element.61), custom_call_target="InvertDiagBlocksLowerTriangular" | custom-call | tf_op jit(solution)/shard_map/jit(_solve_triangular)/triangular_solve | solution.py:38
  3291.2 11.7 cholesky.606
  3303.1 9.8 custom-call.51
  3313.6 12.1 cholesky.625
  3325.7 9.8 custom-call.52
  3336.2 11.7 cholesky.646
  3347.9 9.8 custom-call.53
  3358.4 11.9 cholesky.663
  3374.9 7.9 while.18
  3384.5 39.3 %custom-call.55 = f32[4,128,128]{1,2,0:T(8,128)S(1)} custom-call(f32[4,128,128]{2,1,0:T(8,128)S(1)} %get-tuple-element.63), custom_call_target="InvertDiagBlocksLowerTriangular" | custom-call | tf_op jit(solution)/shard_map/jit(_solve_triangular)/triangular_solve | solution.py:38
  3433.3 11.7 cholesky.678
  3445.2 9.8 custom-call.56
  3455.7 11.9 cholesky.697
  3467.6 9.8 custom-call.57
  3478.1 11.7 cholesky.718
  3489.9 9.8 custom-call.58
  3500.3 12.1 cholesky.735
  3517.4 8.6 while.19
  3527.0 39.3 %custom-call.60 = f32[4,128,128]{1,2,0:T(8,128)S(1)} custom-call(f32[4,128,128]{2,1,0:T(8,128)S(1)} %get-tuple-element.65), custom_call_target="InvertDiagBlocksLowerTriangular" | custom-call | tf_op jit(solution)/shard_map/jit(_solve_triangular)/triangular_solve | solution.py:38
  (546 shorter events, 296.0 us)
Async XLA Ops:
  7.2 795.4 %copy-start.12 = (f32[1,1,6,6]{3,1,2,0:T(1,128)S(1)}, f32[1,1,6,6]{3,1,2,0:T(1,128)}, u32[]{:S(2)}) copy-start(f32[1,1,6,6]{3,1,2,0:T(1,128)} %param.21) | copy-start | bytes 436
  7.2 795.5 %copy-start.49 = (f32[1,1,6,6]{3,1,2,0:T(1,128)S(1)}, f32[1,1,6,6]{3,1,2,0:T(1,128)}, u32[]{:S(2)}) copy-start(f32[1,1,6,6]{3,1,2,0:T(1,128)} %param.20) | copy-start | bytes 436
  7.2 1526.3 %copy-start = (f32[2,1,512,512]{3,2,1,0:T(8,128)S(1)}, f32[2,1,512,512]{3,2,1,0:T(8,128)}, u32[]{:S(2)}) copy-start(f32[2,1,512,512]{3,2,1,0:T(8,128)} %param.14) | copy-start | bytes 6291460
  7.2 302.4 %all-reduce.18.cloned.1.call-start = ((), (), s32[]{:S(2)}) async-start(), calls=%async_computation | async-start | bytes 131072
  10.4 16.7 collective-permute-start.7
  11.7 15.4 collective-permute-start.6
  15.5 9.5 collective-permute-start.5
  23.0 3.4 collective-permute-start.4
  27.1 1531.3 %copy-start.60 = (f32[6]{0:T(128)}, f32[6]{0:T(128)S(1)}, u32[]{:S(2)}) copy-start(f32[6]{0:T(128)S(1)} %bitcast_add_fusion.4) | copy-start | bytes 76
  27.2 9.9 collective-permute-start.9
  34.2 10.4 collective-permute-start.8
  47.4 637.9 %all-reduce.20.cloned.1.call-start = ((), (), s32[]{:S(2)}) async-start(), calls=%async_computation.1 | async-start | bytes 131072
  310.6 469.8 %copy-start.52 = (f32[32]{0:T(128)}, f32[32]{0:T(128)S(1)}, u32[]{:S(2)}) copy-start(f32[32]{0:T(128)S(1)} %div.51) | copy-start | bytes 388
  404.8 750.0 %copy-start.43 = (f32[6,32]{1,0:T(8,128)}, f32[6,32]{1,0:T(8,128)S(1)}, u32[]{:S(2)}) copy-start(f32[6,32]{1,0:T(8,128)S(1)} %multiply_add_fusion.7) | copy-start | bytes 2308
  404.8 4.3 collective-permute-start.11
  406.1 3.8 collective-permute-start.10
  410.0 9.9 collective-permute-start.13
  416.5 10.4 collective-permute-start.12
  429.6 630.0 %all-reduce.22.cloned.1.call-start = ((), (), s32[]{:S(2)}) async-start(), calls=%async_computation.2 | async-start | bytes 131072
  780.5 750.0 %copy-start.33 = (f32[6,32]{1,0:T(8,128)}, f32[6,32]{1,0:T(8,128)S(1)}, u32[]{:S(2)}) copy-start(f32[6,32]{1,0:T(8,128)S(1)} %multiply_add_fusion.6) | copy-start | bytes 2308
  780.5 4.3 collective-permute-start.15
  781.8 3.8 collective-permute-start.14
  785.6 9.9 collective-permute-start.17
  792.1 10.4 collective-permute-start.16
  803.9 630.0 %all-reduce.24.cloned.1.call-start = ((), (), s32[]{:S(2)}) async-start(), calls=%async_computation.3 | async-start | bytes 131072
  1154.8 375.7 %copy-start.35 = (f32[6,32]{1,0:T(8,128)}, f32[6,32]{1,0:T(8,128)S(1)}, u32[]{:S(2)}) copy-start(f32[6,32]{1,0:T(8,128)S(1)} %multiply_add_fusion.5) | copy-start | bytes 2308
  1154.8 4.3 collective-permute-start.19
  1156.1 3.8 collective-permute-start.18
  1160.0 9.9 collective-permute-start.21
  1166.5 10.4 collective-permute-start.20
  1178.2 634.7 %all-reduce.26.cloned.1.call-start = ((), (), s32[]{:S(2)}) async-start(), calls=%async_computation.4 | async-start | bytes 131072
  1529.2 12.1 collective-permute-start.23
  1530.5 10.8 collective-permute-start.22
  1537.3 1440.3 %collective-permute-start = (f32[512,512]{0,1:T(8,128)}, f32[512,512]{0,1:T(8,128)}, u32[]{:S(2)}, u32[]{:S(2)}) collective-permute-start(f32[512,512]{0,1:T(8,128)} %bitcast.1), channel_id=1, source_target_pairs={{0,16},{16,32},{32,48},{48,64},{64,80},{80,96},{96,112},{112,128},... | collective-permute-start | bytes 3145736 | tf_op jit(solution)/shard_map/ppermute | solution.py:13
  1541.3 9.9 collective-permute-start.25
  1547.8 10.4 collective-permute-start.24
  1560.1 630.5 %all-reduce.28.cloned.1.call-start = ((), (), s32[]{:S(2)}) async-start(), calls=%async_computation.5 | async-start | bytes 131072
  1560.8 1556.2 %collective-permute-start.1 = (f32[32,512]{1,0:T(8,128)}, f32[32,512]{1,0:T(8,128)}, u32[]{:S(2)}, u32[]{:S(2)}) collective-permute-start(f32[32,512]{1,0:T(8,128)} %get-tuple-element.134), channel_id=1, source_target_pairs={{0,16},{16,32},{32,48},{48,64},{64,80},{80,96},{96,112},{112,128},... | collective-permute-start | bytes 196616 | tf_op jit(solution)/shard_map/ppermute | solution.py:13
  1564.1 1566.6 %collective-permute-start.2 = (f32[512,512]{0,1:T(8,128)}, f32[512,512]{0,1:T(8,128)S(1)}, u32[]{:S(2)}, u32[]{:S(2)}) collective-permute-start(f32[512,512]{0,1:T(8,128)} %bitcast.539), channel_id=1, source_target_pairs={{16,0},{32,16},{48,32},{64,48},{80,64},{96,80},{112,96},{128,112},... | collective-permute-start | bytes 3145736 | tf_op jit(solution)/shard_map/ppermute | solution.py:13
  1911.4 377.3 %copy-start.39 = (f32[6,32]{1,0:T(8,128)}, f32[6,32]{1,0:T(8,128)S(1)}, u32[]{:S(2)}) copy-start(f32[6,32]{1,0:T(8,128)S(1)} %multiply_add_fusion.3) | copy-start | bytes 2308
  1911.4 7.6 collective-permute-start.27
  1912.8 6.1 collective-permute-start.26
  1918.9 394.7 %copy-start.8 = (f32[1,2,32,512]{3,2,1,0:T(8,128)S(1)}, f32[1,2,32,512]{3,2,1,0:T(8,128)}, u32[]{:S(2)}) copy-start(f32[1,2,32,512]{3,2,1,0:T(8,128)} %param.17) | copy-start | bytes 393220
  1919.0 10.0 collective-permute-start.29
  1925.6 10.4 collective-permute-start.28
  1937.4 631.0 %all-reduce.30.cloned.1.call-start = ((), (), s32[]{:S(2)}) async-start(), calls=%async_computation.6 | async-start | bytes 131072
  2193.9 375.5 %copy-start.59 = (f32[32]{0:T(128)}, f32[32]{0:T(128)S(1)}, u32[]{:S(2)}) copy-start(f32[32]{0:T(128)S(1)} %div.61) | copy-start | bytes 388
  2288.7 378.0 %copy-start.41 = (f32[6,32]{1,0:T(8,128)}, f32[6,32]{1,0:T(8,128)S(1)}, u32[]{:S(2)}) copy-start(f32[6,32]{1,0:T(8,128)S(1)} %multiply_add_fusion.2) | copy-start | bytes 2308
  2288.7 6.0 collective-permute-start.31
  2290.0 4.7 collective-permute-start.30
  2294.7 9.9 collective-permute-start.33
  2301.2 10.4 collective-permute-start.32
  2313.6 660.9 %all-reduce.32.cloned.1.call-start = ((), (), s32[]{:S(2)}) async-start(), calls=%async_computation.7 | async-start | bytes 131072
  2316.6 384.9 %copy-start.51 = (f32[1,1,6,6]{3,1,2,0:T(1,128)S(1)}, f32[1,1,6,6]{3,1,2,0:T(1,128)}, u32[]{:S(2)}) copy-start(f32[1,1,6,6]{3,1,2,0:T(1,128)} %param.20) | copy-start | bytes 436
  2666.7 7.7 collective-permute-start.35
  2668.0 7.7 collective-permute-start.34
  2671.7 308.0 %copy-start.3 = (f32[1,1,512,512]{2,3,1,0:T(8,128)S(1)}, f32[1,1,512,512]{2,3,1,0:T(8,128)}, u32[]{:S(2)}) copy-start(f32[1,1,512,512]{2,3,1,0:T(8,128)} %copy.44) | copy-start | bytes 3145732
  2674.4 605.9 %collective-permute-start.3 = (f32[32,512]{1,0:T(8,128)}, f32[32,512]{1,0:T(8,128)}, u32[]{:S(2)}, u32[]{:S(2)}) collective-permute-start(f32[32,512]{1,0:T(8,128)} %get-tuple-element.135), channel_id=1, source_target_pairs={{16,0},{32,16},{48,32},{64,48},{80,64},{96,80},{112,96},{128,112},... | collective-permute-start | bytes 196616 | tf_op jit(solution)/shard_map/ppermute | solution.py:13
  2676.3 9.5 collective-permute-start.37
  2685.7 10.4 collective-permute-start.36
  2696.1 593.1 %collective-permute-start.38 = (f32[512,512]{0,1:T(8,128)}, f32[512,512]{0,1:T(8,128)}, u32[]{:S(2)}, u32[]{:S(2)}) collective-permute-start(f32[512,512]{0,1:T(8,128)} %bitcast.92), channel_id=1, source_target_pairs={{0,1},{1,2},{2,3},{3,4},{4,5},{5,6},{6,7},{7,8},{8,9},{9,10},{10,1... | collective-permute-start | bytes 3145736 | tf_op jit(solution)/shard_map/ppermute | solution.py:13
  2977.6 446.2 %collective-permute-start.39 = (f32[32,512]{1,0:T(8,128)}, f32[32,512]{1,0:T(8,128)}, u32[]{:S(2)}, u32[]{:S(2)}) collective-permute-start(f32[32,512]{1,0:T(8,128)} %get-tuple-element.130), channel_id=1, source_target_pairs={{0,1},{1,2},{2,3},{3,4},{4,5},{5,6},{6,7},{7,8},{8,9},{9,10},{10,1... | collective-permute-start | bytes 196616 | tf_op jit(solution)/shard_map/ppermute | solution.py:13
  3117.0 314.0 %collective-permute-start.40 = (f32[512,512]{0,1:T(8,128)}, f32[512,512]{0,1:T(8,128)}, u32[]{:S(2)}, u32[]{:S(2)}) collective-permute-start(f32[512,512]{0,1:T(8,128)} %bitcast.538), channel_id=1, source_target_pairs={{1,0},{2,1},{3,2},{4,3},{5,4},{6,5},{7,6},{8,7},{9,8},{10,9},{11,1... | collective-permute-start | bytes 3145736 | tf_op jit(solution)/shard_map/ppermute | solution.py:13
  3130.7 435.7 %collective-permute-start.41 = (f32[32,512]{1,0:T(8,128)}, f32[32,512]{1,0:T(8,128)}, u32[]{:S(2)}, u32[]{:S(2)}) collective-permute-start(f32[32,512]{1,0:T(8,128)} %get-tuple-element.131), channel_id=1, source_target_pairs={{1,0},{2,1},{3,2},{4,3},{5,4},{6,5},{7,6},{8,7},{9,8},{10,9},{11,1... | collective-permute-start | bytes 196616 | tf_op jit(solution)/shard_map/ppermute | solution.py:13
  (52 other events, 3907.8 us)
Sparse Core Ops, SparseCore 0:
  47.5 262.0 all-reduce.17
  429.7 255.4 all-reduce.19
  804.0 255.5 all-reduce.21
  1178.4 255.5 all-reduce.23
  1560.2 252.6 all-reduce.25
  1937.5 253.0 all-reduce.27
  2313.7 254.6 all-reduce.29
  2704.6 269.8 all-reduce.31
